TPU v7x, 128 devices: a whole 4x4x4 slice. The times are simulated.
128 devices in a mesh: expert: 32 (over x, y, z_lo), dp: 4 (over z_hi, core).
Axes of the slice: x: 4, y: 4, z: 4 (z_hi: 2, z_lo: 2; z = z_hi * 2 + z_lo), core: 2. Of those that a mesh axis runs over, the one named last changes fastest.
Arguments:
- tokens: bfloat16 [8192, 5120], P('expert'), may hold values from -6 to 6
- out_grad: bfloat16 [8192, 5120], P('expert'), may hold values from -6 to 6
- assignments: int32 [8192, 6], P('expert'), may hold values from 0 to 159, all different within a row; in each aligned block of 256 rows (0 to 255, 256 to 511, ...) at most 12 rows name the same one
- w_gate: bfloat16 [32, 5120, 768], P('expert', None, 'dp'), may hold values from -0.078125 to 0.078125
- w_up: bfloat16 [32, 5120, 768], P('expert', None, 'dp'), may hold values from -0.078125 to 0.078125
- w_down: bfloat16 [32, 768, 5120], P('expert', 'dp'), may hold values from -0.21875 to 0.21875
Outputs:
- in_grad: bfloat16 [8192, 5120], P('expert', 'dp')
- grad_gate: bfloat16 [32, 5120, 768], P('expert', None, 'dp')
- grad_up: bfloat16 [32, 5120, 768], P('expert', None, 'dp')
- grad_down: bfloat16 [32, 768, 5120], P('expert', 'dp')
Inputs may be any that keep to these rules, and one draw needn't show every extreme that they name: `assignments`: each token names 6 different experts; among the 256 rows of one device (aligned blocks) no expert is named by more than 12 tokens.
All inputs are finite; a program needn't handle non-finite values.
Results may differ from a plain program's by a relative error of at most 0.0054.
Values may be sent and summed in bfloat16 or wider, within the bound.
A program may use at most 128 MiB of HBM per device.

v0:
```python
import jax
import jax.numpy as jnp
from jax import lax
from jax.sharding import PartitionSpec as P

CAP = 12


def expert_back(rows_x, rows_g, gate_w, up_w, down_w):
    a_val = jnp.dot(rows_x, gate_w, preferred_element_type=jnp.float32)
    b_val = jnp.dot(rows_x, up_w, preferred_element_type=jnp.float32)
    s_val = jax.nn.sigmoid(a_val)
    silu_val = a_val * s_val
    hidden = (silu_val * b_val).astype(jnp.bfloat16)
    d_hidden = jnp.einsum("rd,fd->rf", rows_g, down_w, preferred_element_type=jnp.float32)
    d_gate = (d_hidden * b_val * s_val * (1.0 + a_val * (1.0 - s_val))).astype(jnp.bfloat16)
    d_up = (d_hidden * silu_val).astype(jnp.bfloat16)
    g_gate = jnp.einsum("rd,rf->df", rows_x, d_gate, preferred_element_type=jnp.float32)
    g_up = jnp.einsum("rd,rf->df", rows_x, d_up, preferred_element_type=jnp.float32)
    g_down = jnp.einsum("rf,rd->fd", hidden, rows_g, preferred_element_type=jnp.float32)
    terms = jnp.einsum("rf,df->rd", d_gate, gate_w, preferred_element_type=jnp.float32)
    terms = terms + jnp.einsum("rf,df->rd", d_up, up_w, preferred_element_type=jnp.float32)
    return (g_gate, g_up, g_down, terms)


def place_slots(valid, target, token_of, length):
    dest = jnp.where(valid, target, length)
    slot_tok = jnp.zeros((length,), jnp.int32).at[dest].set(token_of, mode="drop")
    slot_on = jnp.zeros((length,), jnp.bool_).at[dest].set(True, mode="drop")
    return (slot_tok, slot_on)


def take_rows(source, slot_tok, slot_on):
    return jnp.where(slot_on[:, None], source[slot_tok], jnp.zeros((), source.dtype))


def per_device(tokens, out_grad, assignments, w_gate, w_up, w_down):
    n_exp = lax.axis_size("expert")
    width = tokens.shape[1]
    tok_count = tokens.shape[0]
    gate_w, up_w, down_w = (w_gate[0], w_up[0], w_down[0])
    picks = assignments.reshape(-1)
    token_of = jnp.arange(picks.shape[0], dtype=jnp.int32) // assignments.shape[1]
    onehot = (picks[:, None] == jnp.arange(n_exp, dtype=jnp.int32)[None, :]).astype(jnp.int32)
    rank = jnp.sum((jnp.cumsum(onehot, axis=0) - onehot) * onehot, axis=1)
    inside = picks < n_exp
    length = n_exp * CAP
    slot_tok, slot_on = place_slots(inside, picks * CAP + rank, token_of, length)
    send_x = take_rows(tokens, slot_tok, slot_on).reshape(n_exp, CAP, width)
    send_g = take_rows(out_grad, slot_tok, slot_on).reshape(n_exp, CAP, width)
    got_x, got_g = (
        lax.all_to_all(send_x, "expert", split_axis=0, concat_axis=0, tiled=True),
        lax.all_to_all(send_g, "expert", split_axis=0, concat_axis=0, tiled=True),
    )
    g_gate, g_up, g_down, terms = expert_back(
        got_x.reshape(length, width), got_g.reshape(length, width), gate_w, up_w, down_w
    )
    back = lax.all_to_all(
        terms.reshape(n_exp, CAP, width), "expert", split_axis=0, concat_axis=0, tiled=True
    )
    pick_rows = lax.psum_scatter(
        back.reshape(length, width), "dp", scatter_dimension=1, tiled=True
    ).astype(jnp.bfloat16)
    combine = (
        (slot_tok[None, :] == jnp.arange(tok_count, dtype=jnp.int32)[:, None]) & slot_on[None, :]
    ).astype(jnp.bfloat16)
    in_grad = jnp.dot(combine, pick_rows, preferred_element_type=jnp.float32).astype(jnp.bfloat16)
    return (
        in_grad,
        g_gate.astype(jnp.bfloat16)[None],
        g_up.astype(jnp.bfloat16)[None],
        g_down.astype(jnp.bfloat16)[None],
    )


def solution(mesh):
    in_specs = (
        P("expert", None),
        P("expert", None),
        P("expert", None),
        P("expert", None, "dp"),
        P("expert", None, "dp"),
        P("expert", "dp", None),
    )
    out_specs = (
        P("expert", "dp"),
        P("expert", None, "dp"),
        P("expert", None, "dp"),
        P("expert", "dp", None),
    )
    return jax.shard_map(
        per_device, mesh=mesh, in_specs=in_specs, out_specs=out_specs, check_vma=False
    )
```

profile of v0, /device:TPU:1, one launch (start us, length us, event | category | flops | bytes accessed | tf_op | source)
XLA Modules:
  0.0 462.2 jit_solution(4294624682766840645)
XLA Ops:
  7.2 0.0 copy-start
  7.2 0.9 broadcast_compare_fusion
  8.0 0.7 broadcast_multiply_fusion
  8.7 0.8 copy.12
  9.6 0.1 eq.42
  9.7 0.1 eq.38
  9.9 0.2 copy.10
  10.0 0.2 lt.33
  10.2 0.1 copy.11
  10.3 0.1 mul.42
  10.5 9.1 %reduce-window.6 = s32[32,12,128]{2,1,0:T(8,128)S(1)} reduce-window(s32[32,12,128]{2,1,0:T(8,128)S(1)} %fusion.16, s32[]{:T(128)} %constant.12.clone.1), window={size=1x1x128 pad=0_0x0_0x127_0}, to_apply=%region_0.1 | reduce-window | flops 6242304 | bytes 393220 | tf_op jit(solution)/shard_map/reduce-window
  19.6 0.1 slice.12
  19.7 0.2 copy.14
  20.0 0.1 copy.15
  20.1 0.1 broadcast_add_fusion
  20.2 0.1 fusion.19
  20.3 6.2 %scatter_custom_fusion = s32[384]{0:T(512)S(1)} fusion(s32[1536]{0:T(1024)S(1)} %fusion.26, s32[1536]{0:T(1024)S(1)} %add_select_fusion, s32[]{:T(128)} %constant.12.clone.1), kind=kCustom, calls=%fused_computation.54 | custom fusion | bytes 1540 | tf_op jit(solution)/shard_map/scatter | solution.py:28
  26.5 11.4 %scatter_custom_fusion.1 = pred[384]{0:T(512)(128)(4,1)S(1)} fusion(s32[1536]{0:T(1024)S(1)} %fusion.26, pred[1536]{0:T(1024)(128)(4,1)S(1)} %broadcast.84, pred[]{:T(512)} %constant.10.clone.1), kind=kCustom, calls=%fused_computation.56 | custom fusion | bytes 385 | tf_op jit(solution)/shard_map/scatter | solution.py:29
  37.9 0.1 broadcast_in_dim.52
  38.1 4.8 %gather_fusion.1 = bf16[384,5120]{1,0:T(8,128)(2,1)} fusion(bf16[256,5120]{1,0:T(8,128)(2,1)S(1)} %copy-done, s32[1024]{0:T(1024)S(1)} %pad_clamp_fusion), kind=kCustom, calls=%fused_computation.1 | custom fusion | bytes 7865856 | tf_op jit(solution)/shard_map/gather | solution.py:34
  42.8 7.1 %gather.13 = bf16[32,12,5120]{2,1,0:T(8,128)(2,1)} reshape(bf16[384,5120]{1,0:T(8,128)(2,1)} %gather_fusion.1) | data formatting | bytes 7864320 | tf_op jit(solution)/shard_map/gather | solution.py:34
  49.9 4.6 %gather_fusion = bf16[384,5120]{1,0:T(8,128)(2,1)} fusion(bf16[256,5120]{1,0:T(8,128)(2,1)S(1)} %copy-done.2, s32[1024]{0:T(1024)S(1)} %pad_clamp_fusion), kind=kCustom, calls=%fused_computation | custom fusion | bytes 7865856 | tf_op jit(solution)/shard_map/gather | solution.py:34
  54.6 7.0 %gather.11 = bf16[32,12,5120]{2,1,0:T(8,128)(2,1)} reshape(bf16[384,5120]{1,0:T(8,128)(2,1)} %gather_fusion) | data formatting | bytes 7864320 | tf_op jit(solution)/shard_map/gather | solution.py:34
  61.5 8.8 %broadcast_select_fusion.1 = (bf16[32,12,5120]{2,1,0:T(8,128)(2,1)}, bf16[32,12,5120]{2,1,0:T(8,128)(2,1)}) fusion(bf16[32,12,5120]{2,1,0:T(8,128)(2,1)} %gather.11, pred[32,12]{1,0:T(8,128)(4,1)S(1)} %broadcast_in_dim.52, bf16[32,12,5120]{2,1,0:T(8,128)(2,1)} %gather.13), kind=kLoop, calls=%fused_computation.12 | loop fusion | flops 3932160 | bytes 15729024 | tf_op jit(solution)/shard_map/jit(_where)/select_n | solution.py:34
  70.3 70.3 %all_to_all.15 = bf16[32,12,5120]{2,1,0:T(8,128)(2,1)} all-to-all(bf16[32,12,5120]{2,1,0:T(8,128)(2,1)} %get-tuple-element.7), channel_id=1, replica_groups=mesh['expert'=32,'dp'=4] {'expert'}, dimensions={0} | all-to-all | bytes 7864320 | tf_op jit(solution)/shard_map/all_to_all | solution.py:52
  140.7 4.9 %all-to-all-start = ((bf16[32,12,5120]{2,1,0:T(8,128)(2,1)}), bf16[32,12,5120]{2,1,0:T(8,128)(2,1)}, u32[]{:S(2)}, u32[]{:S(2)}) async-start(bf16[32,12,5120]{2,1,0:T(8,128)(2,1)} %get-tuple-element.6), calls=%async_computation | async-start | bytes 10485760 | tf_op jit(solution)/shard_map/all_to_all | solution.py:53
  145.5 0.0 copy-start.6
  145.5 0.0 reduce-scatter.2.cloned.1.call-start
  145.6 7.2 %reshape.98 = bf16[384,5120]{1,0:T(8,128)(2,1)} reshape(bf16[32,12,5120]{2,1,0:T(8,128)(2,1)} %all_to_all.15) | data formatting | bytes 7864320 | tf_op jit(solution)/shard_map/reshape | solution.py:56
  152.8 3.7 fusion.5
  156.5 0.2 copy-done.7
  156.7 1.5 fusion.8
  158.2 56.1 %all-to-all-done = bf16[32,12,5120]{2,1,0:T(8,128)(2,1)} async-done(((bf16[32,12,5120]{2,1,0:T(8,128)(2,1)}), bf16[32,12,5120]{2,1,0:T(8,128)(2,1)}, u32[]{:S(2)}, u32[]{:S(2)}) %all-to-all-start) | async-done | bytes 3932192 | tf_op jit(solution)/shard_map/all_to_all | solution.py:53
  214.2 7.1 %reshape.97 = bf16[384,5120]{1,0:T(8,128)(2,1)} reshape(bf16[32,12,5120]{2,1,0:T(8,128)(2,1)} %all-to-all-done) | data formatting | bytes 7864320 | tf_op jit(solution)/shard_map/reshape | solution.py:56
  221.3 4.2 multiply_convert_fusion.1
  225.5 0.0 copy-start.8
  225.5 1.2 fusion.3
  226.7 0.3 copy-done.8
  227.0 4.4 convolution_add_fusion
  231.4 9.2 %reshape.99 = f32[32,12,5120]{2,1,0:T(8,128)} reshape(f32[384,5120]{1,0:T(8,128)} %convolution_add_fusion) | data formatting | bytes 15728640 | tf_op jit(solution)/shard_map/reshape | solution.py:59
  240.6 124.4 %all_to_all.16 = f32[32,12,5120]{2,1,0:T(8,128)} all-to-all(f32[32,12,5120]{2,1,0:T(8,128)} %reshape.99), channel_id=1, replica_groups=mesh['expert'=32,'dp'=4] {'expert'}, dimensions={0} | all-to-all | bytes 15728640 | tf_op jit(solution)/shard_map/all_to_all | solution.py:58
  364.9 9.4 %reshape.100 = f32[384,5120]{1,0:T(8,128)} reshape(f32[32,12,5120]{2,1,0:T(8,128)} %all_to_all.16) | data formatting | bytes 15728640 | tf_op jit(solution)/shard_map/reshape | solution.py:62
  374.3 0.0 reduce-scatter.2.cloned.1.call-update
  374.3 4.7 %fusion.2 = bf16[1,5120,192]{1,2,0:T(8,128)(2,1)} fusion(bf16[384,192]{0,1:T(8,128)(2,1)S(1)} %get-tuple-element.4, bf16[384,5120]{1,0:T(8,128)(2,1)} %reshape.98), kind=kOutput, calls=%fused_computation.10 | convolution fusion | flops 755957760 | bytes 6045696 | tf_op jit(solution)/shard_map/rd,rf->df/dot_general | solution.py:19
  379.1 2.5 fusion.1
  381.6 2.5 fusion
  384.1 68.5 %reduce-scatter.2.cloned.1.call-done = f32[384,1280]{1,0:T(8,128)} async-done(((f32[384,5120]{1,0:T(8,128)}), f32[384,1280]{1,0:T(8,128)}) %reduce-scatter.2.cloned.1.call-update) | async-done | bytes 1966096 | tf_op jit(solution)/shard_map/reduce_scatter | solution.py:61
  452.5 2.9 convolution_convert_fusion.3
  (20 shorter events, 0.1 us)
Async XLA Ops:
  7.2 30.9 %copy-start = (bf16[256,5120]{1,0:T(8,128)(2,1)S(1)}, bf16[256,5120]{1,0:T(8,128)(2,1)}, u32[]{:S(2)}) copy-start(bf16[256,5120]{1,0:T(8,128)(2,1)} %param.6) | copy-start | bytes 7864324
  42.8 7.1 %copy-start.2 = (bf16[256,5120]{1,0:T(8,128)(2,1)S(1)}, bf16[256,5120]{1,0:T(8,128)(2,1)}, u32[]{:S(2)}) copy-start(bf16[256,5120]{1,0:T(8,128)(2,1)} %param.7) | copy-start | bytes 7864324
  140.7 73.6 %all-to-all-start = ((bf16[32,12,5120]{2,1,0:T(8,128)(2,1)}), bf16[32,12,5120]{2,1,0:T(8,128)(2,1)}, u32[]{:S(2)}, u32[]{:S(2)}) async-start(bf16[32,12,5120]{2,1,0:T(8,128)(2,1)} %get-tuple-element.6), calls=%async_computation | async-start | bytes 10485760 | tf_op jit(solution)/shard_map/all_to_all | solution.py:53
  145.5 7.2 %copy-start.6 = (bf16[1,5120,192]{1,2,0:T(8,128)(2,1)S(1)}, bf16[1,5120,192]{1,2,0:T(8,128)(2,1)}, u32[]{:S(2)}) copy-start(bf16[1,5120,192]{1,2,0:T(8,128)(2,1)} %param.9) | copy-start | bytes 5898244
  145.5 307.0 %reduce-scatter.2.cloned.1.call-start = ((), (), s32[]{:S(2)}) async-start(), calls=%async_computation.4 | async-start | bytes 9830400 | tf_op jit(solution)/shard_map/reduce_scatter | solution.py:61
  152.8 3.7 copy-start.3
  152.8 3.9 copy-start.7
  225.5 1.5 copy-start.8
  374.3 4.7 %copy-start.4 = (bf16[384,5120]{1,0:T(8,128)(2,1)S(1)}, bf16[384,5120]{1,0:T(8,128)(2,1)}, u32[]{:S(2)}) copy-start(bf16[384,5120]{1,0:T(8,128)(2,1)} %reshape.98) | copy-start | bytes 11796484
  379.1 2.5 copy-start.5
  379.1 76.3 %copy-start.1 = (bf16[256,5120]{1,0:T(8,128)(2,1)S(1)}, bf16[256,5120]{1,0:T(8,128)(2,1)}, u32[]{:S(2)}) copy-start(bf16[256,5120]{1,0:T(8,128)(2,1)} %param.6) | copy-start | bytes 7864324
Sparse Core Ops, SparseCore 0:
  374.4 78.0 reduce-scatter.1
where the time goes:
time: 464 us; the launch traced here: 462 us
  blocking collectives  195 us (42%)
  waiting for transfers between devices  125 us (27%)
  local copies, waits for them, and re-layouts  76.6 us (17%)
  matrix products  27.5 us (6%)
  other arithmetic  19.7 us (4%)
  between operations  14.2 us (3%)
  starting transfers between devices  4.9 us (1%)
    all_to_all x1, blocking collectives, per_device(): lax.all_to_all(terms.reshape(n_exp, CAP, width), 'expert', split_axis=0,...  124 us
    all_to_all x1, blocking collectives, per_device(): lax.all_to_all(send_x, 'expert', split_axis=0, concat_axis=0, tiled=True)  70.3 us
    reduce_scatter x1, waiting for transfers between devices, per_device(): lax.psum_scatter(back.reshape(length, width), 'dp', scatter_dimension=1,...  68.5 us
    all_to_all x1, waiting for transfers between devices, per_device(): lax.all_to_all(send_g, 'expert', split_axis=0, concat_axis=0, tiled=True)  56.1 us
    gather x4, local copies, waits for them, and re-layouts, take_rows(): source[slot_tok]  23.5 us
    scatter x1, local copies, waits for them, and re-layouts, place_slots(): slot_on = jnp.zeros((length,), jnp.bool_).at[dest].set(True, mode='drop')  11.4 us
    reshape x1, local copies, waits for them, and re-layouts, per_device(): back.reshape(length, width)  9.37 us
  transfers between devices with their start and end apart: 2, of which 2 were waited for; matrix products, arithmetic and copies ran while one was open for 5% of the time, Pallas kernels for 0%

commit v1 on v0

v1 whole, which is shorter than its diff:
```python
import functools

import jax
import jax.numpy as jnp
from jax import lax
from jax.experimental import pallas as pl
from jax.experimental.pallas import tpu as pltpu
from jax.sharding import PartitionSpec as P

MESH = pl.DeviceIdType.MESH
BF, F32 = jnp.bfloat16, jnp.float32

D, FL, CAP, TOK = 5120, 192, 12, 256
Q, E8 = D // 4, D // 8
CHUNKS = (
    ((1, 2), (3, 2), (2, 1), (2, 3)),
    ((2, 0), (0, 2), (0, 0), (2, 2)),
    ((1, 1), (3, 3), (1, 3), (3, 1)),
    ((1, 0), (3, 0), (0, 1), (0, 3)),
)
NC = len(CHUNKS)
G = 4
B = G * CAP
M = G * B
R = 2 * B


def mm(a, b):
    return lax.dot_general(a, b, (((1,), (0,)), ((), ())), preferred_element_type=F32)


def mm_nt(a, b):
    return lax.dot_general(a, b, (((1,), (1,)), ((), ())), preferred_element_type=F32)


def mm_tn(a, b):
    return lax.dot_general(a, b, (((0,), (0,)), ((), ())), preferred_element_type=F32)


def iota(shape, dim):
    return lax.broadcasted_iota(jnp.int32, shape, dim)


def kernel(
    tok_hbm, grad_hbm, assign_ref, wg_hbm, wu_hbm, wd_hbm,
    in_hbm, gg_hbm, gu_hbm, gd_hbm,
    src, wg, wu, wd, codes, smat, perm, wide,
    pk_n, pk_c, rn, rc_relay, rc, rows, own, ex_send, ex_recv,
    z_send, z_recv, ret_send, ret_recv, unp, da_s, db_s, h_s,
    o_gg, o_gu, o_gd, o_in,
    ld_sem, out_sem, self_sem,
    pn_s, pn_r, pc_s, pc_r, zf_s, zf_r, sn_s, sn_r, sc_s, sc_r,
    ex_s, ex_r, zr_s, zr_r, rt_s, rt_r,
):
    e_idx, d_idx = lax.axis_index("expert"), lax.axis_index("dp")
    x, y, zl = e_idx // 8, (e_idx // 2) % 4, e_idx % 2
    zh, c = d_idx // 2, d_idx % 2

    def column(dx, dy):
        return ((x + dx) % 4) * 4 + (y + dy) % 4

    def plane(dx, dy):
        return (column(dx, dy) * 2 + zl, d_idx)

    def z_side(w):
        return ((x * 4 + y) * 2 + (1 - zl), 2 * w + c)

    z_far = (e_idx, 2 * (1 - zh) + c)
    sibling = (e_idx, 2 * zh + (1 - c))

    def remote(a, b, s, r, dev):
        return pltpu.make_async_remote_copy(
            src_ref=a, dst_ref=b, send_sem=s, recv_sem=r, device_id=dev, device_id_type=MESH
        )

    @pl.when(c == 0)
    def _():
        pltpu.make_async_copy(tok_hbm, src, ld_sem.at[0]).start()

    @pl.when(c == 1)
    def _():
        pltpu.make_async_copy(grad_hbm, src, ld_sem.at[0]).start()

    loads = [
        pltpu.make_async_copy(wg_hbm.at[0], wg, ld_sem.at[1]),
        pltpu.make_async_copy(wu_hbm.at[0], wu, ld_sem.at[2]),
        pltpu.make_async_copy(wd_hbm.at[0], wd, ld_sem.at[3]),
    ]
    barrier = pltpu.get_barrier_semaphore()
    offsets = [o for ch in CHUNKS for o in ch]
    partners = [plane(*o) for o in offsets if o != (0, 0)]
    partners += [z_side(0), z_side(1), z_far, sibling]
    for dev in partners:
        pl.semaphore_signal(barrier, inc=1, device_id=dev, device_id_type=MESH)

    lane = iota((TOK, 128), 1)
    member = jnp.zeros((TOK, 128), F32)
    for k in range(assign_ref.shape[1]):
        member = member + jnp.where(assign_ref[:, k : k + 1] == lane, 1.0, 0.0)
    member = member.astype(BF)
    t0, t1 = iota((TOK, TOK), 0), iota((TOK, TOK), 1)
    upto = jnp.where(t0 <= t1, 1.0, 0.0).astype(BF)
    eye = jnp.where(t0 == t1, 1.0, 0.0).astype(BF)
    codes[...] = mm_tn(member, eye) * mm_tn(member, upto)
    row = iota((B, TOK), 0)
    grp, want = row // CAP, (row % CAP + 1).astype(F32)
    for k in range(NC):
        for kind in range(2):
            z_of = zl if kind == 0 else 1 - zl
            code = jnp.zeros((B, TOK), F32)
            for i, o in enumerate(CHUNKS[k]):
                line = codes[pl.ds(column(*o) * 2 + z_of, 1), :]
                code = jnp.where(grp == i, jnp.broadcast_to(line, (B, TOK)), code)
            smat[k, kind * B : (kind + 1) * B, :] = jnp.where(code == want, 1.0, 0.0).astype(BF)
    r0, r1 = iota((M, M), 0), iota((M, M), 1)
    swapped = ((r0 // CAP) % 4) * B + (r0 // B) * CAP + r0 % CAP
    perm[...] = jnp.where(swapped == r1, 1.0, 0.0).astype(BF)

    pl.semaphore_wait(barrier, len(partners))
    pltpu.make_async_copy(tok_hbm, src, ld_sem.at[0]).wait()
    for load in loads:
        load.start()

    def slot(k, i):
        return pl.ds(k * M + i * B, B)

    def chunk(k):
        return pl.ds(k * M, M)

    def send_n(k, i):
        return remote(pk_n.at[slot(k, i)], rn.at[c, slot(k, i)], pn_s.at[k * G + i], pn_r.at[k * G + i],
                      plane(*CHUNKS[k][i]))

    def send_c(k, i):
        return remote(pk_c.at[slot(k, i)], rc_relay.at[slot(k, i)], pc_s.at[k * G + i], pc_r.at[k * G + i],
                      plane(*CHUNKS[k][i]))

    def self_copies(k, i):
        return (
            pltpu.make_async_copy(pk_n.at[slot(k, i)], rn.at[c, slot(k, i)], self_sem.at[0]),
            pltpu.make_async_copy(pk_c.at[slot(k, i)], rc_relay.at[slot(k, i)], self_sem.at[1]),
        )

    def pack(k):
        for q in range(4):
            cols = pl.ds(q * Q, Q)
            wide[:, cols] = mm(smat[k], src[:, cols]).astype(BF)
        stack_n = jnp.concatenate([wide[0:B, q * Q : (q + 1) * Q] for q in range(4)], axis=0)
        pk_n[chunk(k), :] = mm(perm[...], stack_n).astype(BF)
        stack_c = jnp.concatenate(
            [wide[B:R, pl.ds(pl.multiple_of(zh * (D // 2) + j * E8, 128), E8)] for j in range(4)], axis=0
        )
        pk_c[chunk(k), :] = mm(perm[...], stack_c).astype(BF)
        for i, o in enumerate(CHUNKS[k]):
            if o == (0, 0):
                for cp in self_copies(k, i):
                    cp.start()
            else:
                send_n(k, i).start()
                send_c(k, i).start()

    def z_forward(k, w):
        return remote(rc_relay.at[chunk(k)], rc.at[c, zh, chunk(k)], zf_s.at[k * 2 + w], zf_r.at[k * 2 + zh],
                      z_side(w))

    def z_forward_in(k, w):
        return remote(rc_relay.at[chunk(k)], rc.at[c, w, chunk(k)], zf_s.at[k * 2 + w], zf_r.at[k * 2 + w],
                      z_side(w))

    def core_n(k, a):
        return remote(rn.at[a, chunk(k)], rn.at[a, chunk(k)], sn_s.at[k], sn_r.at[k], sibling)

    def core_c(k, a, w):
        return remote(rc.at[a, w, chunk(k)], rc.at[a, w, chunk(k)], sc_s.at[k * 2 + w], sc_r.at[k * 2 + w], sibling)

    def arrive(k):
        for i, o in enumerate(CHUNKS[k]):
            if o == (0, 0):
                for cp in self_copies(k, i):
                    cp.wait()
            else:
                send_n(k, i).wait_recv()
                send_c(k, i).wait_recv()
        for w in range(2):
            z_forward(k, w).start()
        core_n(k, c).start()

    def relay(k):
        for w in range(2):
            z_forward_in(k, w).wait_recv()
            core_c(k, c, w).start()

    def compute(k):
        core_n(k, 1 - c).wait_recv()
        for w in range(2):
            core_c(k, 1 - c, w).wait_recv()
        base = k * R
        for a in range(2):
            flat = mm(perm[...], rn[a, chunk(k), :]).astype(BF)
            for q in range(4):
                rows[a, base : base + B, q * Q : (q + 1) * Q] = flat[q * B : (q + 1) * B]
            for w in range(2):
                flat = mm(perm[...], rc[a, w, chunk(k), :]).astype(BF)
                for j in range(4):
                    at = w * (D // 2) + j * E8
                    rows[a, base + B : base + R, at : at + E8] = flat[j * B : (j + 1) * B]

        def forward(q, acc):
            cols = pl.ds(pl.multiple_of(q * Q, 128), Q)
            xt = rows[0, pl.ds(base, R), cols]
            gt = rows[1, pl.ds(base, R), cols]
            return (
                acc[0] + mm(xt, wg[cols, :]),
                acc[1] + mm(xt, wu[cols, :]),
                acc[2] + mm_nt(gt, wd[:, cols]),
            )

        zero = jnp.zeros((R, FL), F32)
        a_v, b_v, dh = lax.fori_loop(0, 4, forward, (zero, zero, zero))
        s_v = jax.nn.sigmoid(a_v)
        silu = a_v * s_v
        h_s[base : base + R, :] = (silu * b_v).astype(BF)
        da = (dh * b_v * s_v * (1.0 + a_v * (1.0 - s_v))).astype(BF)
        db = (dh * silu).astype(BF)
        da_s[base : base + R, :] = da
        db_s[base : base + R, :] = db

        def terms(w, core):
            at = pl.ds(pl.multiple_of((2 * w + core) * Q, 128), Q)
            return mm_nt(da, wg[at, :]) + mm_nt(db, wu[at, :])

        for w in range(2):
            ex_send[k, w] = terms(w, 1 - c).astype(BF)
        core_ex(k).start()
        for w in range(2):
            own[k % 2, w] = terms(w, c)

    def core_ex(k):
        return remote(ex_send.at[k], ex_recv.at[k], ex_s.at[k], ex_r.at[k], sibling)

    def z_far_copy(k):
        return remote(z_send.at[k, 0], z_recv.at[k, 0], zr_s.at[k * 3], zr_r.at[k * 3], z_far)

    def z_side_copy(k, w):
        return remote(z_send.at[k, 1 + w], z_recv.at[k, 1 + zh], zr_s.at[k * 3 + 1 + w], zr_r.at[k * 3 + 1 + zh],
                      z_side(w))

    def z_side_in(k, w):
        return remote(z_send.at[k, 1 + w], z_recv.at[k, 1 + w], zr_s.at[k * 3 + 1 + w], zr_r.at[k * 3 + 1 + w],
                      z_side(w))

    def z_reduce(k):
        core_ex(k).wait_recv()
        p = k % 2
        far = own[p, 1 - zh, 0:B, :] + ex_recv[k, 1 - zh, 0:B, :].astype(F32)
        z_send[k, 0] = far.astype(BF)
        z_far_copy(k).start()
        for w in range(2):
            z_send[k, 1 + w] = (own[p, w, B:R, :] + ex_recv[k, w, B:R, :].astype(F32)).astype(BF)
            z_side_copy(k, w).start()

    def back(k, i):
        dx, dy = CHUNKS[k][i]
        return remote(ret_send.at[slot(k, i)], ret_recv.at[slot(k, i)], rt_s.at[k * G + i], rt_r.at[k * G + i],
                      plane(-dx, -dy))

    def self_back(k, i):
        return pltpu.make_async_copy(ret_send.at[slot(k, i)], ret_recv.at[slot(k, i)], self_sem.at[2])

    def give_back(k):
        p = k % 2
        z_far_copy(k).wait_recv()
        mine = own[p, zh, 0:B, :] + ex_recv[k, zh, 0:B, :].astype(F32) + z_recv[k, 0].astype(F32)
        for w in range(2):
            z_side_in(k, w).wait_recv()
        side = z_recv[k, 1].astype(F32) + z_recv[k, 2].astype(F32)
        mine, side = mine.astype(BF), side.astype(BF)
        stack = jnp.concatenate([mine[:, :E8], side[:, :E8], mine[:, E8:], side[:, E8:]], axis=0)
        ret_send[chunk(k), :] = mm(perm[...], stack).astype(BF)
        for i, o in enumerate(CHUNKS[k]):
            if o == (0, 0):
                self_back(k, i).start()
            else:
                back(k, i).start()

    def collect(k):
        for i, o in enumerate(CHUNKS[k]):
            if o == (0, 0):
                self_back(k, i).wait()
            else:
                back(k, i).wait_recv()
        flat = mm(perm[...], ret_recv[chunk(k), :]).astype(BF)
        for hf in range(2):
            unp[k * R : (k + 1) * R, hf * E8 : (hf + 1) * E8] = flat[hf * R : (hf + 1) * R]

    outs = [
        pltpu.make_async_copy(o_gg, gg_hbm.at[0], out_sem.at[0]),
        pltpu.make_async_copy(o_gu, gu_hbm.at[0], out_sem.at[1]),
        pltpu.make_async_copy(o_gd, gd_hbm.at[0], out_sem.at[2]),
        pltpu.make_async_copy(o_in, in_hbm, out_sem.at[3]),
    ]

    def weight_grads():
        @pl.loop(0, 10)
        def _(t):
            cols = pl.ds(pl.multiple_of(t * 512, 128), 512)
            xt = rows[0, :, cols]
            o_gg[cols, :] = mm_tn(xt, da_s[...]).astype(BF)
            o_gu[cols, :] = mm_tn(xt, db_s[...]).astype(BF)
            o_gd[:, cols] = mm_tn(h_s[...], rows[1, :, cols]).astype(BF)

        for cp in outs[:3]:
            cp.start()

    for k in range(NC):
        pack(k)
    for load in loads:
        load.wait()
    for k in range(NC + 2):
        if k < NC:
            arrive(k)
        if 0 <= k - 1 < NC:
            relay(k - 1)
            compute(k - 1)
            z_reduce(k - 1)
        if k == NC:
            give_back(k - 2)
            weight_grads()
        elif 0 <= k - 2 < NC:
            give_back(k - 2)
    for k in range(NC):
        collect(k)
    smat_all = smat[...].reshape(NC * R, TOK)
    o_in[...] = mm_tn(smat_all, unp[...]).astype(BF)
    outs[3].start()

    for k in range(NC):
        for i, o in enumerate(CHUNKS[k]):
            if o != (0, 0):
                send_n(k, i).wait_send()
                send_c(k, i).wait_send()
                back(k, i).wait_send()
        for w in range(2):
            z_forward(k, w).wait_send()
            core_c(k, c, w).wait_send()
            z_side_copy(k, w).wait_send()
        core_n(k, c).wait_send()
        core_ex(k).wait_send()
        z_far_copy(k).wait_send()
    for cp in outs:
        cp.wait()


def per_device(tokens, out_grad, assignments, w_gate, w_up, w_down):
    hbm = pl.BlockSpec(memory_space=pl.ANY)
    vmem = pl.BlockSpec(memory_space=pltpu.VMEM)
    S = pltpu.SemaphoreType.DMA
    bf = lambda *shape: pltpu.VMEM(shape, BF)
    scratch = [
        bf(TOK, D), bf(D, FL), bf(D, FL), bf(FL, D),
        pltpu.VMEM((128, TOK), F32), bf(NC, R, TOK), bf(M, M), bf(R, D),
        bf(NC * M, Q), bf(NC * M, E8), bf(2, NC * M, Q), bf(NC * M, E8), bf(2, 2, NC * M, E8),
        bf(2, NC * R, D), pltpu.VMEM((2, 2, R, Q), F32), bf(NC, 2, R, Q), bf(NC, 2, R, Q),
        bf(NC, 3, B, Q), bf(NC, 3, B, Q), bf(NC * M, E8), bf(NC * M, E8), bf(NC * R, Q),
        bf(NC * R, FL), bf(NC * R, FL), bf(NC * R, FL),
        bf(D, FL), bf(D, FL), bf(FL, D), bf(TOK, Q),
        S((4,)), S((4,)), S((3,)),
        S((NC * G,)), S((NC * G,)), S((NC * G,)), S((NC * G,)),
        S((NC * 2,)), S((NC * 2,)), S((NC,)), S((NC,)), S((NC * 2,)), S((NC * 2,)),
        S((NC,)), S((NC,)), S((NC * 3,)), S((NC * 3,)), S((NC * G,)), S((NC * G,)),
    ]
    return tuple(pl.pallas_call(
        kernel,
        out_shape=(
            jax.ShapeDtypeStruct((TOK, Q), BF),
            jax.ShapeDtypeStruct((1, D, FL), BF),
            jax.ShapeDtypeStruct((1, D, FL), BF),
            jax.ShapeDtypeStruct((1, FL, D), BF),
        ),
        in_specs=[hbm, hbm, vmem, hbm, hbm, hbm],
        out_specs=(hbm, hbm, hbm, hbm),
        scratch_shapes=scratch,
        compiler_params=pltpu.CompilerParams(
            collective_id=0, has_side_effects=True, vmem_limit_bytes=62 * 2**20
        ),
        cost_estimate=pl.CostEstimate(flops=7 * 10**9, bytes_accessed=17 * 10**6, transcendentals=73728),
    )(tokens, out_grad, assignments, w_gate, w_up, w_down))


def solution(mesh):
    in_specs = (
        P("expert", None),
        P("expert", None),
        P("expert", None),
        P("expert", None, "dp"),
        P("expert", None, "dp"),
        P("expert", "dp", None),
    )
    out_specs = (
        P("expert", "dp"),
        P("expert", None, "dp"),
        P("expert", None, "dp"),
        P("expert", "dp", None),
    )
    return jax.shard_map(
        per_device, mesh=mesh, in_specs=in_specs, out_specs=out_specs, check_vma=False
    )
```

time: 464 us -> 113 us (0.24)
  blocking collectives: 195 us -> 0 us
  waiting for transfers between devices: 125 us -> 0 us
  Pallas kernels: 0 us -> 92.5 us
  local copies, waits for them, and re-layouts: 76.6 us -> 19 us
  matrix products: 27.5 us -> 0 us
  other arithmetic: 19.7 us -> 0 us
  between operations: 14.2 us -> 0.65 us
  starting transfers between devices: 4.9 us -> 0 us
    all_to_all x2 -> x0, blocking collectives: 195 us -> none  [the longest x1 124 us: per_device(): lax.all_to_all(terms.reshape(n_exp, CAP, width), 'expert', split_axis=0,...]
    pallas_call x0 -> x1, Pallas kernels: none -> 92.5 us  [per_device(): pl.pallas_call(kernel, out_shape=(jax.ShapeDtypeStruct((TOK, Q), BF), jax...]
    reduce_scatter x1 -> x0, waiting for transfers between devices: 68.5 us -> none  [per_device(): lax.psum_scatter(back.reshape(length, width), 'dp', scatter_dimension=1,...]
    all_to_all x1 -> x0, waiting for transfers between devices: 56.1 us -> none  [per_device(): lax.all_to_all(send_g, 'expert', split_axis=0, concat_axis=0, tiled=True)]
    reshape x4 -> x0, local copies, waits for them, and re-layouts: 32.8 us -> none  [the longest x1 9.37 us: per_device(): back.reshape(length, width)]
    dot_general x9 -> x0, matrix products: 27.5 us -> none  [the longest x1 4.73 us: expert_back(): jnp.einsum('rd,rf->df', rows_x, d_up, preferred_element_type=jnp.float32)]
    gather x4 -> x0, local copies, waits for them, and re-layouts: 23.5 us -> none  [take_rows(): source[slot_tok]]
    scatter x2 -> x0, local copies, waits for them, and re-layouts: 17.6 us -> none  [the longest x1 11.4 us: place_slots(): slot_on = jnp.zeros((length,), jnp.bool_).at[dest].set(True, mode='drop')]
  transfers between devices with their start and end apart: 2 -> 0, of which waited for: 2 -> 0; matrix products, arithmetic and copies ran while one was open for 5% -> 0% of each run, Pallas kernels for 0% -> 0%
where the time goes in v1:
time: 113 us; the launch traced here: 112 us
  Pallas kernels  92.5 us (82%)
  local copies, waits for them, and re-layouts  19 us (17%)
    pallas_call x1, Pallas kernels, per_device(): pl.pallas_call(kernel, out_shape=(jax.ShapeDtypeStruct((TOK, Q), BF), jax...  92.5 us
    unnamed x11, local copies, waits for them, and re-layouts  12.2 us
    pallas_call x2, local copies, waits for them, and re-layouts, per_device(): pl.pallas_call(kernel, out_shape=(jax.ShapeDtypeStruct((TOK, Q), BF), jax...  6.76 us

profile of v1, /device:TPU:1, one launch (start us, length us, event | category | flops | bytes accessed | tf_op | source)
XLA Modules:
  0.0 112.1 jit_solution(1583728405584624406)
XLA Ops:
  0.6 1.5 %copy.10.assign_ref = s32[256,6]{1,0:T(8,128)} copy(s32[256,6]{0,1:T(8,128)} %param.8) | data formatting | bytes 12288 | tf_op args[2]
  2.1 0.0 copy-start.1
  2.1 4.4 %copy.11.wg_hbm = bf16[1,5120,192]{2,1,0:T(8,128)(2,1)} copy(bf16[1,5120,192]{1,2,0:T(8,128)(2,1)} %param.9) | data formatting | bytes 3932160 | tf_op args[3]
  6.5 0.0 copy-done.1
  6.5 2.5 %copy.12.wu_hbm = bf16[1,5120,192]{2,1,0:T(8,128)(2,1)} copy(bf16[1,5120,192]{1,2,0:T(8,128)(2,1)S(1)} %copy-done.1) | data formatting | bytes 3932160 | tf_op args[4]
  9.1 92.5 %shard_map.93 = (bf16[256,1280]{1,0:T(8,128)(2,1)}, bf16[1,5120,192]{2,1,0:T(8,128)(2,1)}, bf16[1,5120,192]{2,1,0:T(8,128)(2,1)}, bf16[1,192,5120]{2,1,0:T(8,128)(2,1)}) custom-call(bf16[256,5120]{1,0:T(8,128)(2,1)} %tok_hbm.1, bf16[256,5120]{1,0:T(8,128)(2,1)} %grad_hbm.1, s32[256,6]{1,0:T(8,128)} %copy.10.assign_ref, bf16[1,5120,192]{2,1,0:T(8,128)(2,1)} %copy.11.wg_hbm, ...), custom_call_target="tpu_custom_call" | custom-call | flops 7000000000 | bytes 17000000 | tf_op jit(solution)/shard_map/pallas_call | solution.py:372
  101.6 0.0 copy-start
  101.6 4.4 %copy.13 = bf16[1,5120,192]{1,2,0:T(8,128)(2,1)} copy(bf16[1,5120,192]{2,1,0:T(8,128)(2,1)} %get-tuple-element.5) | data formatting | bytes 3932160 | tf_op jit(solution)/shard_map/pallas_call | solution.py:372
  106.0 0.0 copy-done
  106.0 0.0 copy-start.2
  106.0 2.4 %copy.14 = bf16[1,5120,192]{1,2,0:T(8,128)(2,1)} copy(bf16[1,5120,192]{2,1,0:T(8,128)(2,1)S(1)} %copy-done) | data formatting | bytes 3932160 | tf_op jit(solution)/shard_map/pallas_call | solution.py:372
  108.4 0.0 copy-done.2
  108.4 0.8 copy.17
  109.2 2.9 %copy.18 = bf16[1,192,5120]{2,1,0:T(8,128)(2,1)} copy(bf16[1,192,5120]{2,1,0:T(8,128)(2,1)} %get-tuple-element.15) | data formatting | bytes 3932160
Async XLA Ops:
  2.1 4.4 %copy-start.1 = (bf16[1,5120,192]{1,2,0:T(8,128)(2,1)S(1)}, bf16[1,5120,192]{1,2,0:T(8,128)(2,1)}, u32[]{:S(2)}) copy-start(bf16[1,5120,192]{1,2,0:T(8,128)(2,1)} %param.10) | copy-start | bytes 5898244
  101.6 4.4 %copy-start = (bf16[1,5120,192]{2,1,0:T(8,128)(2,1)S(1)}, bf16[1,5120,192]{2,1,0:T(8,128)(2,1)}, u32[]{:S(2)}) copy-start(bf16[1,5120,192]{2,1,0:T(8,128)(2,1)} %get-tuple-element.6) | copy-start | bytes 5898244
  106.0 2.4 %copy-start.2 = (bf16[256,1280]{1,0:T(8,128)(2,1)S(1)}, bf16[256,1280]{1,0:T(8,128)(2,1)}, u32[]{:S(2)}) copy-start(bf16[256,1280]{1,0:T(8,128)(2,1)} %get-tuple-element.12) | copy-start | bytes 1966084

commit v2 on v1

v2 whole, which is shorter than its diff:
```python
import functools

import jax
import jax.numpy as jnp
from jax import lax
from jax.experimental import pallas as pl
from jax.experimental.pallas import tpu as pltpu
from jax.sharding import PartitionSpec as P

MESH = pl.DeviceIdType.MESH
BF, F32 = jnp.bfloat16, jnp.float32

D, FL, FP, CAP, TOK = 5120, 192, 256, 12, 256
Q, E8 = D // 4, D // 8
N_EXP = 32
CHUNKS = (
    ((1, 0), (3, 0), (0, 1), (0, 3)),
    ((1, 2), (3, 2), (2, 1), (2, 3)),
    ((1, 1), (3, 3), (1, 3), (3, 1)),
    ((2, 0), (0, 2), (0, 0), (2, 2)),
)
NC = len(CHUNKS)
G = 4
B = G * CAP
M = G * B
R = 2 * B
ALL = 2 * NC * B


def mm(a, b):
    return lax.dot_general(a, b, (((1,), (0,)), ((), ())), preferred_element_type=F32)


def mm_nt(a, b):
    return lax.dot_general(a, b, (((1,), (1,)), ((), ())), preferred_element_type=F32)


def mm_tn(a, b):
    return lax.dot_general(a, b, (((0,), (0,)), ((), ())), preferred_element_type=F32)


def iota(shape, dim):
    return lax.broadcasted_iota(jnp.int32, shape, dim)


def kernel(
    tok_hbm, grad_hbm, assign_ref, wg_hbm, wu_hbm, wd_hbm,
    o_in, o_gg, o_gu, o_gd,
    src, w_all, wt, codes, smat, perm, wide,
    pk_n, pk_c, rn, rc_relay, rc, rows, own, ex_send, ex_recv,
    zc_send, zc_recv, zn_send, zn_recv, ret_send, ret_recv, unp, dab_s, h_s, lhs,
    ld_sem, self_sem,
    pn_s, pn_r, pc_s, pc_r, zf_s, zf_r, sn_s, sn_r, sc_s, sc_r,
    ex_s, ex_r, zc_s, zc_r, zn_s, zn_r, rt_s, rt_r,
):
    e_idx, d_idx = lax.axis_index("expert"), lax.axis_index("dp")
    x, y, zl = e_idx // 8, (e_idx // 2) % 4, e_idx % 2
    zh, c = d_idx // 2, d_idx % 2

    def column(dx, dy):
        return ((x + dx) % 4) * 4 + (y + dy) % 4

    def plane(dx, dy):
        return (column(dx, dy) * 2 + zl, d_idx)

    def z_side(w):
        return ((x * 4 + y) * 2 + (1 - zl), 2 * w + c)

    z_far = (e_idx, 2 * (1 - zh) + c)
    sibling = (e_idx, 2 * zh + (1 - c))

    def remote(a, b, s, r, dev):
        return pltpu.make_async_remote_copy(
            src_ref=a, dst_ref=b, send_sem=s, recv_sem=r, device_id=dev, device_id_type=MESH
        )

    @pl.when(c == 0)
    def _():
        pltpu.make_async_copy(tok_hbm, src, ld_sem.at[0]).start()

    @pl.when(c == 1)
    def _():
        pltpu.make_async_copy(grad_hbm, src, ld_sem.at[0]).start()

    loads = [
        pltpu.make_async_copy(wg_hbm.at[0], w_all.at[pl.ds(0, FL)], ld_sem.at[1]),
        pltpu.make_async_copy(wu_hbm.at[0], w_all.at[pl.ds(FP, FL)], ld_sem.at[2]),
        pltpu.make_async_copy(wd_hbm.at[0], o_gd, ld_sem.at[3]),
    ]
    barrier = pltpu.get_barrier_semaphore()
    offsets = [o for ch in CHUNKS for o in ch]
    partners = [plane(*o) for o in offsets if o != (0, 0)]
    partners += [z_side(0), z_side(1), z_far, sibling]
    for dev in partners:
        pl.semaphore_signal(barrier, inc=1, device_id=dev, device_id_type=MESH)

    expert = iota((N_EXP, TOK), 0)
    member = jnp.zeros((N_EXP, TOK), F32)
    for k in range(assign_ref.shape[0]):
        member = member + jnp.where(assign_ref[k : k + 1, :] == expert, 1.0, 0.0)
    upto = jnp.where(iota((TOK, TOK), 0) <= iota((TOK, TOK), 1), 1.0, 0.0).astype(BF)
    codes[...] = member * mm(member.astype(BF), upto)
    row = iota((B, TOK), 0)
    grp, want = row // CAP, (row % CAP + 1).astype(F32)
    for kind in range(2):
        z_of = 1 - zl if kind == 0 else zl
        for k in range(NC):
            code = jnp.zeros((B, TOK), F32)
            for i, o in enumerate(CHUNKS[k]):
                line = codes[pl.ds(column(*o) * 2 + z_of, 1), :]
                code = jnp.where(grp == i, jnp.broadcast_to(line, (B, TOK)), code)
            at = (kind * NC + k) * B
            smat[at : at + B, :] = jnp.where(code == want, 1.0, 0.0).astype(BF)
    r0, r1 = iota((M, M), 0), iota((M, M), 1)
    swapped = ((r0 // CAP) % 4) * B + (r0 // B) * CAP + r0 % CAP
    perm[...] = jnp.where(swapped == r1, 1.0, 0.0).astype(BF)

    pl.semaphore_wait(barrier, len(partners))
    pltpu.make_async_copy(tok_hbm, src, ld_sem.at[0]).wait()
    for load in loads:
        load.start()
    for a in range(2):
        w_all[a * FP + FL : (a + 1) * FP, :] = jnp.zeros((FP - FL, D), BF)

    def slot(k, i):
        return pl.ds(k * M + i * B, B)

    def chunk(k):
        return pl.ds(k * M, M)

    def send_n(k, i):
        return remote(pk_n.at[slot(k, i)], rn.at[c, slot(k, i)], pn_s.at[k * G + i], pn_r.at[k * G + i],
                      plane(*CHUNKS[k][i]))

    def send_c(k, i):
        return remote(pk_c.at[slot(k, i)], rc_relay.at[slot(k, i)], pc_s.at[k * G + i], pc_r.at[k * G + i],
                      plane(*CHUNKS[k][i]))

    def self_n(k, i):
        return pltpu.make_async_copy(pk_n.at[slot(k, i)], rn.at[c, slot(k, i)], self_sem.at[0])

    def self_c(k, i):
        return pltpu.make_async_copy(pk_c.at[slot(k, i)], rc_relay.at[slot(k, i)], self_sem.at[1])

    def pack_c():
        for j in range(4):
            cols = pl.ds(pl.multiple_of(zh * (D // 2) + j * E8, 128), E8)
            wide[:, j * E8 : (j + 1) * E8] = mm(smat[0:M, :], src[:, cols]).astype(BF)
        for k in range(NC):
            stack = jnp.concatenate(
                [wide[k * B : (k + 1) * B, j * E8 : (j + 1) * E8] for j in range(4)], axis=0
            )
            pk_c[chunk(k), :] = mm(perm[...], stack).astype(BF)

    def pack_n():
        for q in range(4):
            wide[:, q * Q : (q + 1) * Q] = mm(smat[M : 2 * M, :], src[:, q * Q : (q + 1) * Q]).astype(BF)
        for k in range(NC):
            stack = jnp.concatenate([wide[k * B : (k + 1) * B, q * Q : (q + 1) * Q] for q in range(4)], axis=0)
            pk_n[chunk(k), :] = mm(perm[...], stack).astype(BF)

    def go(k, far, near):
        for i, o in enumerate(CHUNKS[k]):
            (near if o == (0, 0) else far)(k, i).start()

    def sent(k, far):
        for i, o in enumerate(CHUNKS[k]):
            if o != (0, 0):
                far(k, i).wait_send()

    def come(k, far, near):
        for i, o in enumerate(CHUNKS[k]):
            if o == (0, 0):
                near(k, i).wait()
            else:
                far(k, i).wait_recv()

    def go_c(k):
        go(k, send_c, self_c)

    def go_n(k):
        go(k, send_n, self_n)

    def sent_c(k):
        sent(k, send_c)

    def sent_n(k):
        sent(k, send_n)

    def z_forward(k, w):
        return remote(rc_relay.at[chunk(k)], rc.at[c, zh, chunk(k)], zf_s.at[k * 2 + w], zf_r.at[k * 2 + zh],
                      z_side(w))

    def z_forward_in(k, w):
        return remote(rc_relay.at[chunk(k)], rc.at[c, w, chunk(k)], zf_s.at[k * 2 + w], zf_r.at[k * 2 + w],
                      z_side(w))

    def core_n(k, a):
        return remote(rn.at[a, chunk(k)], rn.at[a, chunk(k)], sn_s.at[k], sn_r.at[k], sibling)

    def core_c(k, a, w):
        return remote(rc.at[a, w, chunk(k)], rc.at[a, w, chunk(k)], sc_s.at[k * 2 + w], sc_r.at[k * 2 + w], sibling)

    def arrive_c(k):
        come(k, send_c, self_c)
        for w in range(2):
            z_forward(k, w).start()

    def arrive_n(k):
        come(k, send_n, self_n)
        core_n(k, c).start()

    def relay(k):
        for w in range(2):
            z_forward_in(k, w).wait_recv()
            core_c(k, c, w).start()

    def unpack(kind, pair):
        base = (kind * 2 + pair) * R
        for half in range(2):
            k, at = pair * 2 + half, base + half * B
            if kind == 1:
                core_n(k, 1 - c).wait_recv()
                for a in range(2):
                    flat = mm(perm[...], rn[a, chunk(k), :]).astype(BF)
                    for q in range(4):
                        rows[a, at : at + B, q * Q : (q + 1) * Q] = flat[q * B : (q + 1) * B]
            else:
                for w in range(2):
                    core_c(k, 1 - c, w).wait_recv()
                for a in range(2):
                    for w in range(2):
                        flat = mm(perm[...], rc[a, w, chunk(k), :]).astype(BF)
                        for j in range(4):
                            col = w * (D // 2) + j * E8
                            rows[a, at : at + B, col : col + E8] = flat[j * B : (j + 1) * B]

    def hidden(kind, pair):
        base = (kind * 2 + pair) * R

        def forward(q, acc):
            cols = pl.ds(pl.multiple_of(q * Q, 128), Q)
            xt = rows[0, pl.ds(base, R), cols]
            gt = rows[1, pl.ds(base, R), cols]
            return (
                acc[0] + mm(xt, wt[cols, 0 : 2 * FP]),
                acc[1] + mm(gt, wt[cols, 2 * FP : 3 * FP]),
            )

        ab, dh = lax.fori_loop(0, 4, forward, (jnp.zeros((R, 2 * FP), F32), jnp.zeros((R, FP), F32)))
        a_v, b_v = ab[:, :FP], ab[:, FP:]
        s_v = jax.nn.sigmoid(a_v)
        silu = a_v * s_v
        h_s[base : base + R, :] = (silu * b_v).astype(BF)
        dab_s[base : base + R, :FP] = (dh * b_v * s_v * (1.0 + a_v * (1.0 - s_v))).astype(BF)
        dab_s[base : base + R, FP:] = (dh * silu).astype(BF)

    def terms(kind, pair):
        group = kind * 2 + pair
        base = group * R

        def term(w, core):
            at = pl.ds(pl.multiple_of((2 * w + core) * Q, 128), Q)
            return mm(dab_s[base : base + R, :], w_all[0 : 2 * FP, at])

        for w in range(2):
            ex_send[group, w] = term(w, 1 - c).astype(BF)
        core_ex(group).start()
        for w in range(2):
            own[pair, w] = term(w, c)

    def core_ex(group):
        return remote(ex_send.at[group], ex_recv.at[group], ex_s.at[group], ex_r.at[group], sibling)

    def z_far_copy(pair):
        return remote(zn_send.at[pair], zn_recv.at[pair], zn_s.at[pair], zn_r.at[pair], z_far)

    def z_side_copy(pair, w):
        return remote(zc_send.at[pair, w], zc_recv.at[pair, zh], zc_s.at[pair * 2 + w], zc_r.at[pair * 2 + zh],
                      z_side(w))

    def z_side_in(pair, w):
        return remote(zc_send.at[pair, w], zc_recv.at[pair, w], zc_s.at[pair * 2 + w], zc_r.at[pair * 2 + w],
                      z_side(w))

    def z_reduce(kind, pair):
        group = kind * 2 + pair
        core_ex(group).wait_recv()
        if kind == 1:
            zn_send[pair] = (own[pair, 1 - zh] + ex_recv[group, 1 - zh].astype(F32)).astype(BF)
            z_far_copy(pair).start()
        else:
            for w in range(2):
                zc_send[pair, w] = (own[pair, w] + ex_recv[group, w].astype(F32)).astype(BF)
                z_side_copy(pair, w).start()

    def z_come(pair):
        for w in range(2):
            z_side_in(pair, w).wait_recv()
        z_far_copy(pair).wait_recv()

    def back(k, i):
        dx, dy = CHUNKS[k][i]
        return remote(ret_send.at[slot(k, i)], ret_recv.at[slot(k, i)], rt_s.at[k * G + i], rt_r.at[k * G + i],
                      plane(-dx, -dy))

    def self_back(k, i):
        return pltpu.make_async_copy(ret_send.at[slot(k, i)], ret_recv.at[slot(k, i)], self_sem.at[2])

    def give_back(k):
        pair, at = k // 2, pl.ds((k % 2) * B, B)
        mine = own[pair, zh, at, :] + ex_recv[2 + pair, zh, at, :].astype(F32) + zn_recv[pair, at, :].astype(F32)
        side = zc_recv[pair, 0, at, :].astype(F32) + zc_recv[pair, 1, at, :].astype(F32)
        mine, side = mine.astype(BF), side.astype(BF)
        stack = jnp.concatenate([mine[:, :E8], side[:, :E8], mine[:, E8:], side[:, E8:]], axis=0)
        ret_send[chunk(k), :] = mm(perm[...], stack).astype(BF)
        go(k, back, self_back)

    def collect(k):
        come(k, back, self_back)
        flat = mm(perm[...], ret_recv[chunk(k), :]).astype(BF)
        for hf in range(2):
            for kind in range(2):
                at, of = (kind * NC + k) * B, (hf * 2 + 1 - kind) * B
                unp[at : at + B, hf * E8 : (hf + 1) * E8] = flat[of : of + B]

    def turn_weights(part):
        loads[part].wait()
        tail = jnp.zeros((FP - FL, 512), BF)

        @pl.loop(0, 10)
        def _(t):
            cols = pl.ds(pl.multiple_of(t * 512, 128), 512)
            mine = o_gd[:, cols] if part == 2 else w_all[part * FP : part * FP + FL, cols]
            full = jnp.concatenate([mine, tail], axis=0)
            wt[cols, part * FP : (part + 1) * FP] = full.T

    def turn_rows():
        lhs[0 : 2 * FP, :] = dab_s[...].astype(F32).T.astype(BF)
        lhs[2 * FP : 3 * FP, :] = h_s[...].astype(F32).T.astype(BF)
        lhs[3 * FP :, :] = smat[...].astype(F32).T.astype(BF)

    def wgrads(first, last):
        @pl.loop(first, last)
        def _(t):
            cols = pl.ds(pl.multiple_of(t * 512, 128), 512)
            both = mm(lhs[0 : 2 * FP, :], rows[0, :, cols])
            o_gg[:, cols] = both[0:FL].astype(BF)
            o_gu[:, cols] = both[FP : FP + FL].astype(BF)
            o_gd[:, cols] = mm(lhs[2 * FP : 3 * FP, :], rows[1, :, cols])[0:FL].astype(BF)

    pack_c()
    go_c(0)
    pack_n()
    sent_c(0)
    go_c(1)
    arrive_c(0)
    turn_weights(0)
    turn_weights(1)
    sent_c(1)
    go_c(2)
    go_c(3)
    arrive_c(1)
    turn_weights(2)
    sent_c(2)
    sent_c(3)
    go_n(0)
    go_n(1)
    arrive_c(2)
    arrive_c(3)
    relay(0)
    relay(1)
    go_n(2)
    go_n(3)
    unpack(0, 0)
    hidden(0, 0)
    terms(0, 0)
    relay(2)
    z_reduce(0, 0)
    relay(3)
    arrive_n(0)
    arrive_n(1)
    unpack(0, 1)
    hidden(0, 1)
    terms(0, 1)
    unpack(1, 0)
    z_reduce(0, 1)
    hidden(1, 0)
    terms(1, 0)
    arrive_n(2)
    arrive_n(3)
    z_reduce(1, 0)
    unpack(1, 1)
    hidden(1, 1)
    terms(1, 1)
    z_reduce(1, 1)
    z_come(0)
    give_back(0)
    give_back(1)
    turn_rows()
    wgrads(0, 5)
    z_come(1)
    give_back(2)
    give_back(3)
    wgrads(5, 10)
    for k in range(NC):
        collect(k)
    o_in[...] = mm(lhs[3 * FP :, :], unp[...]).astype(BF)

    for k in range(NC):
        sent_n(k)
    for k in range(NC):
        sent(k, back)
        for w in range(2):
            z_forward(k, w).wait_send()
            core_c(k, c, w).wait_send()
        core_n(k, c).wait_send()
        core_ex(k).wait_send()
    for pair in range(2):
        for w in range(2):
            z_side_copy(pair, w).wait_send()
        z_far_copy(pair).wait_send()


def hand_over(n, *refs):
    src, dst, sem = refs[:n], refs[n : 2 * n], refs[2 * n]
    outs = [
        pltpu.make_async_copy(src[i], dst[i] if i == 0 else dst[i].at[0], sem.at[i]) for i in range(n)
    ]
    for cp in outs:
        cp.start()
    for cp in outs:
        cp.wait()


def per_device(tokens, out_grad, assignments, w_gate, w_up, w_down):
    hbm = pl.BlockSpec(memory_space=pl.ANY)
    vmem = pl.BlockSpec(memory_space=pltpu.VMEM)
    S = pltpu.SemaphoreType.DMA
    bf = lambda *shape: pltpu.VMEM(shape, BF)
    scratch = [
        bf(TOK, D), bf(2 * FP, D), bf(D, 3 * FP),
        pltpu.VMEM((N_EXP, TOK), F32), bf(ALL, TOK), bf(M, M), bf(M, D),
        bf(NC * M, Q), bf(NC * M, E8), bf(2, NC * M, Q), bf(NC * M, E8), bf(2, 2, NC * M, E8),
        bf(2, ALL, D), pltpu.VMEM((2, 2, R, Q), F32), bf(NC, 2, R, Q), bf(NC, 2, R, Q),
        bf(2, 2, R, Q), bf(2, 2, R, Q), bf(2, R, Q), bf(2, R, Q), bf(NC * M, E8), bf(NC * M, E8), bf(ALL, Q),
        bf(ALL, 2 * FP), bf(ALL, FP), bf(4 * FP, ALL),
        S((4,)), S((3,)),
        S((NC * G,)), S((NC * G,)), S((NC * G,)), S((NC * G,)),
        S((NC * 2,)), S((NC * 2,)), S((NC,)), S((NC,)), S((NC * 2,)), S((NC * 2,)),
        S((NC,)), S((NC,)), S((4,)), S((4,)), S((2,)), S((2,)), S((NC * G,)), S((NC * G,)),
    ]
    made = lambda *shape: jax.ShapeDtypeStruct(shape, BF)
    made_here = pl.pallas_call(
        kernel,
        out_shape=(bf(TOK, Q), bf(FL, D), bf(FL, D), bf(FL, D)),
        in_specs=[hbm, hbm, vmem, hbm, hbm, hbm],
        out_specs=(vmem,) * 4,
        scratch_shapes=scratch,
        compiler_params=pltpu.CompilerParams(
            collective_id=0, has_side_effects=True, vmem_limit_bytes=56 * 2**20
        ),
        cost_estimate=pl.CostEstimate(flops=8 * 10**9, bytes_accessed=15 * 10**6, transcendentals=73728),
    )(tokens, out_grad, assignments.T, w_gate.swapaxes(1, 2), w_up.swapaxes(1, 2), w_down)
    in_grad, g_gate, g_up, g_down = pl.pallas_call(
        functools.partial(hand_over, 4),
        out_shape=(made(TOK, Q), made(1, FL, D), made(1, FL, D), made(1, FL, D)),
        in_specs=[vmem] * 4,
        out_specs=(hbm,) * 4,
        scratch_shapes=[S((4,))],
        compiler_params=pltpu.CompilerParams(vmem_limit_bytes=2 * 2**20),
                cost_estimate=pl.CostEstimate(flops=0, bytes_accessed=7 * 10**6, transcendentals=0),
    )(*[pltpu.with_memory_space_constraint(a, pltpu.VMEM) for a in made_here])
    return in_grad, g_gate.swapaxes(1, 2), g_up.swapaxes(1, 2), g_down


def solution(mesh):
    in_specs = (
        P("expert", None),
        P("expert", None),
        P("expert", None),
        P("expert", None, "dp"),
        P("expert", None, "dp"),
        P("expert", "dp", None),
    )
    out_specs = (
        P("expert", "dp"),
        P("expert", None, "dp"),
        P("expert", None, "dp"),
        P("expert", "dp", None),
    )
    return jax.shard_map(
        per_device, mesh=mesh, in_specs=in_specs, out_specs=out_specs, check_vma=False
    )
```

time: 113 us -> 81.3 us (0.72)
  local copies, waits for them, and re-layouts: 19 us -> 0 us
  Pallas kernels: 92.5 us -> 79.8 us
    pallas_call x1 -> x2, Pallas kernels: 92.5 us -> 79.8 us  [the longest x1 77 us: per_device(): pl.pallas_call(kernel, out_shape=(bf(TOK, Q), bf(FL, D), bf(FL, D), bf(FL...]
    unnamed x11 -> x0, local copies, waits for them, and re-layouts: 12.2 us -> none
    pallas_call x2 -> x0, local copies, waits for them, and re-layouts: 6.76 us -> none  [per_device(): pl.pallas_call(kernel, out_shape=(jax.ShapeDtypeStruct((TOK, Q), BF), jax...]
where the time goes in v2:
time: 81.3 us; the launch traced here: 80.6 us
  Pallas kernels  79.8 us (98%)
    pallas_call x1, Pallas kernels, per_device(): pl.pallas_call(kernel, out_shape=(bf(TOK, Q), bf(FL, D), bf(FL, D), bf(FL...  77 us
    pallas_call x1, Pallas kernels, per_device(): pl.pallas_call(functools.partial(hand_over, 4), out_shape=(made(TOK, Q),...  2.82 us

profile of v2, /device:TPU:1, one launch (start us, length us, event | category | flops | bytes accessed | tf_op | source)
XLA Modules:
  0.0 80.6 jit_solution(15154675467765503727)
XLA Ops:
  0.6 77.0 %shard_map.93 = (bf16[256,1280]{1,0:T(8,128)(2,1)S(1)}, bf16[192,5120]{1,0:T(8,128)(2,1)S(1)}, bf16[192,5120]{1,0:T(8,128)(2,1)S(1)}, bf16[192,5120]{1,0:T(8,128)(2,1)S(1)}) custom-call(bf16[256,5120]{1,0:T(8,128)(2,1)} %tok_hbm.1, bf16[256,5120]{1,0:T(8,128)(2,1)} %grad_hbm.1, s32[6,256]{1,0:T(8,128)} %bitcast.9, bf16[1,192,5120]{2,1,0:T(8,128)(2,1)} %bitcast.5, ...), custom_call_target="tpu_custom_call" | custom-call | flops 8000000000 | bytes 15000000 | tf_op jit(solution)/shard_map/pallas_call | solution.py:454
  77.6 2.8 %shard_map.94 = (bf16[256,1280]{1,0:T(8,128)(2,1)}, bf16[1,192,5120]{2,1,0:T(8,128)(2,1)}, bf16[1,192,5120]{2,1,0:T(8,128)(2,1)}, bf16[1,192,5120]{2,1,0:T(8,128)(2,1)}) custom-call(bf16[256,1280]{1,0:T(8,128)(2,1)S(1)} %get-tuple-element.12.refs_0_, bf16[192,5120]{1,0:T(8,128)(2,1)S(1)} %get-tuple-element.13.refs_1_, ...), custom_call_target="tpu_custom_call" | custom-call | bytes 7000000 | tf_op jit(solution)/shard_map/pallas_call | solution.py:465

commit v3 on v2

--- a/solution.py
+++ b/solution.py
@@ -13,17 +13,19 @@
 D, FL, FP, CAP, TOK = 5120, 192, 256, 12, 256
 Q, E8 = D // 4, D // 8
 N_EXP = 32
+PARTS = 4
 CHUNKS = (
-    ((1, 0), (3, 0), (0, 1), (0, 3)),
-    ((1, 2), (3, 2), (2, 1), (2, 3)),
     ((1, 1), (3, 3), (1, 3), (3, 1)),
     ((2, 0), (0, 2), (0, 0), (2, 2)),
+    ((1, 2), (3, 2), (2, 1), (2, 3)),
+    ((1, 0), (3, 0), (0, 1), (0, 3)),
 )
 NC = len(CHUNKS)
 G = 4
 B = G * CAP
 M = G * B
 R = 2 * B
+EX = ((0, R, 0), (R, R, 1), (2 * R, R, 2), (3 * R, B, 3), (3 * R + B, B, 4))
 ALL = 2 * NC * B
 
 
@@ -102,15 +104,17 @@
     codes[...] = member * mm(member.astype(BF), upto)
     row = iota((B, TOK), 0)
     grp, want = row // CAP, (row % CAP + 1).astype(F32)
-    for kind in range(2):
+
+    def choose(kind, k):
         z_of = 1 - zl if kind == 0 else zl
-        for k in range(NC):
-            code = jnp.zeros((B, TOK), F32)
-            for i, o in enumerate(CHUNKS[k]):
-                line = codes[pl.ds(column(*o) * 2 + z_of, 1), :]
-                code = jnp.where(grp == i, jnp.broadcast_to(line, (B, TOK)), code)
-            at = (kind * NC + k) * B
-            smat[at : at + B, :] = jnp.where(code == want, 1.0, 0.0).astype(BF)
+        code = jnp.zeros((B, TOK), F32)
+        for i, o in enumerate(CHUNKS[k]):
+            line = codes[pl.ds(column(*o) * 2 + z_of, 1), :]
+            code = jnp.where(grp == i, jnp.broadcast_to(line, (B, TOK)), code)
+        at = (kind * NC + k) * B
+        smat[at : at + B, :] = jnp.where(code == want, 1.0, 0.0).astype(BF)
+
+    choose(0, 0)
     r0, r1 = iota((M, M), 0), iota((M, M), 1)
     swapped = ((r0 // CAP) % 4) * B + (r0 // B) * CAP + r0 % CAP
     perm[...] = jnp.where(swapped == r1, 1.0, 0.0).astype(BF)
@@ -142,15 +146,13 @@
     def self_c(k, i):
         return pltpu.make_async_copy(pk_c.at[slot(k, i)], rc_relay.at[slot(k, i)], self_sem.at[1])
 
-    def pack_c():
+    def pack_c(k):
+        at = slice(k * B, (k + 1) * B)
         for j in range(4):
             cols = pl.ds(pl.multiple_of(zh * (D // 2) + j * E8, 128), E8)
-            wide[:, j * E8 : (j + 1) * E8] = mm(smat[0:M, :], src[:, cols]).astype(BF)
-        for k in range(NC):
-            stack = jnp.concatenate(
-                [wide[k * B : (k + 1) * B, j * E8 : (j + 1) * E8] for j in range(4)], axis=0
-            )
-            pk_c[chunk(k), :] = mm(perm[...], stack).astype(BF)
+            wide[at, j * E8 : (j + 1) * E8] = mm(smat[at, :], src[:, cols]).astype(BF)
+        stack = jnp.concatenate([wide[at, j * E8 : (j + 1) * E8] for j in range(4)], axis=0)
+        pk_c[chunk(k), :] = mm(perm[...], stack).astype(BF)
 
     def pack_n():
         for q in range(4):
@@ -215,9 +217,9 @@
             z_forward_in(k, w).wait_recv()
             core_c(k, c, w).start()
 
-    def unpack(kind, pair):
+    def unpack(kind, pair, halves=(0, 1)):
         base = (kind * 2 + pair) * R
-        for half in range(2):
+        for half in halves:
             k, at = pair * 2 + half, base + half * B
             if kind == 1:
                 core_n(k, 1 - c).wait_recv()
@@ -235,45 +237,48 @@
                             col = w * (D // 2) + j * E8
                             rows[a, at : at + B, col : col + E8] = flat[j * B : (j + 1) * B]
 
-    def hidden(kind, pair):
-        base = (kind * 2 + pair) * R
+    def hidden(base, m):
 
         def forward(q, acc):
             cols = pl.ds(pl.multiple_of(q * Q, 128), Q)
-            xt = rows[0, pl.ds(base, R), cols]
-            gt = rows[1, pl.ds(base, R), cols]
+            xt = rows[0, pl.ds(base, m), cols]
+            gt = rows[1, pl.ds(base, m), cols]
             return (
                 acc[0] + mm(xt, wt[cols, 0 : 2 * FP]),
                 acc[1] + mm(gt, wt[cols, 2 * FP : 3 * FP]),
             )
 
-        ab, dh = lax.fori_loop(0, 4, forward, (jnp.zeros((R, 2 * FP), F32), jnp.zeros((R, FP), F32)))
+        ab, dh = lax.fori_loop(0, 4, forward, (jnp.zeros((m, 2 * FP), F32), jnp.zeros((m, FP), F32)))
         a_v, b_v = ab[:, :FP], ab[:, FP:]
         s_v = jax.nn.sigmoid(a_v)
         silu = a_v * s_v
-        h_s[base : base + R, :] = (silu * b_v).astype(BF)
-        dab_s[base : base + R, :FP] = (dh * b_v * s_v * (1.0 + a_v * (1.0 - s_v))).astype(BF)
-        dab_s[base : base + R, FP:] = (dh * silu).astype(BF)
-
-    def terms(kind, pair):
-        group = kind * 2 + pair
-        base = group * R
+        h_s[base : base + m, :] = (silu * b_v).astype(BF)
+        dab_s[base : base + m, :FP] = (dh * b_v * s_v * (1.0 + a_v * (1.0 - s_v))).astype(BF)
+        dab_s[base : base + m, FP:] = (dh * silu).astype(BF)
+
+    def terms(base, m, part):
+        group, lo = base // R, base % R
+        at_rows = slice(lo, lo + m)
 
         def term(w, core):
             at = pl.ds(pl.multiple_of((2 * w + core) * Q, 128), Q)
-            return mm(dab_s[base : base + R, :], w_all[0 : 2 * FP, at])
+            return mm(dab_s[base : base + m, :], w_all[0 : 2 * FP, at])
 
         for w in range(2):
-            ex_send[group, w] = term(w, 1 - c).astype(BF)
-        core_ex(group).start()
+            ex_send[group, w, at_rows] = term(w, 1 - c).astype(BF)
+        core_ex(base, m, part).start()
         for w in range(2):
-            own[pair, w] = term(w, c)
-
-    def core_ex(group):
-        return remote(ex_send.at[group], ex_recv.at[group], ex_s.at[group], ex_r.at[group], sibling)
-
-    def z_far_copy(pair):
-        return remote(zn_send.at[pair], zn_recv.at[pair], zn_s.at[pair], zn_r.at[pair], z_far)
+            own[group % 2, w, at_rows] = term(w, c)
+
+    def core_ex(base, m, part):
+        group, at = base // R, pl.ds(base % R, m)
+        return remote(ex_send.at[group, :, at], ex_recv.at[group, :, at], ex_s.at[part], ex_r.at[part], sibling)
+
+    def z_far_copy(k):
+        return remote(zn_send.at[k], zn_recv.at[k], zn_s.at[k], zn_r.at[k], z_far)
+
+    def go_far(k):
+        z_far_copy(k).start()
 
     def z_side_copy(pair, w):
         return remote(zc_send.at[pair, w], zc_recv.at[pair, zh], zc_s.at[pair * 2 + w], zc_r.at[pair * 2 + zh],
@@ -283,21 +288,20 @@
         return remote(zc_send.at[pair, w], zc_recv.at[pair, w], zc_s.at[pair * 2 + w], zc_r.at[pair * 2 + w],
                       z_side(w))
 
-    def z_reduce(kind, pair):
-        group = kind * 2 + pair
-        core_ex(group).wait_recv()
-        if kind == 1:
-            zn_send[pair] = (own[pair, 1 - zh] + ex_recv[group, 1 - zh].astype(F32)).astype(BF)
-            z_far_copy(pair).start()
-        else:
-            for w in range(2):
-                zc_send[pair, w] = (own[pair, w] + ex_recv[group, w].astype(F32)).astype(BF)
-                z_side_copy(pair, w).start()
-
-    def z_come(pair):
+    def come_ex(part):
+        core_ex(*EX[part]).wait_recv()
+
+    def reduce_side(pair):
+        group = pair
+        core_ex(group * R, R, group).wait_recv()
         for w in range(2):
-            z_side_in(pair, w).wait_recv()
-        z_far_copy(pair).wait_recv()
+            zc_send[pair, w] = (own[pair, w] + ex_recv[group, w].astype(F32)).astype(BF)
+            z_side_copy(pair, w).start()
+
+    def reduce_far(k):
+        pair, at = k // 2, pl.ds((k % 2) * B, B)
+        far = own[pair, 1 - zh, at, :] + ex_recv[2 + pair, 1 - zh, at, :].astype(F32)
+        zn_send[k] = far.astype(BF)
 
     def back(k, i):
         dx, dy = CHUNKS[k][i]
@@ -309,7 +313,11 @@
 
     def give_back(k):
         pair, at = k // 2, pl.ds((k % 2) * B, B)
-        mine = own[pair, zh, at, :] + ex_recv[2 + pair, zh, at, :].astype(F32) + zn_recv[pair, at, :].astype(F32)
+        if k % 2 == 0:
+            for w in range(2):
+                z_side_in(pair, w).wait_recv()
+        z_far_copy(k).wait_recv()
+        mine = own[pair, zh, at, :] + ex_recv[2 + pair, zh, at, :].astype(F32) + zn_recv[k].astype(F32)
         side = zc_recv[pair, 0, at, :].astype(F32) + zc_recv[pair, 1, at, :].astype(F32)
         mine, side = mine.astype(BF), side.astype(BF)
         stack = jnp.concatenate([mine[:, :E8], side[:, :E8], mine[:, E8:], side[:, E8:]], axis=0)
@@ -335,98 +343,125 @@
             full = jnp.concatenate([mine, tail], axis=0)
             wt[cols, part * FP : (part + 1) * FP] = full.T
 
+    def total():
+        o_in[...] = mm(lhs[3 * FL :, :], unp[...]).astype(BF)
+
     def turn_rows():
-        lhs[0 : 2 * FP, :] = dab_s[...].astype(F32).T.astype(BF)
-        lhs[2 * FP : 3 * FP, :] = h_s[...].astype(F32).T.astype(BF)
-        lhs[3 * FP :, :] = smat[...].astype(F32).T.astype(BF)
+        for a in range(2):
+            lhs[a * FL : (a + 1) * FL, :] = dab_s[:, a * FP : (a + 1) * FP].astype(F32).T[0:FL].astype(BF)
+        lhs[2 * FL : 3 * FL, :] = h_s[...].astype(F32).T[0:FL].astype(BF)
+        lhs[3 * FL :, :] = smat[...].astype(F32).T.astype(BF)
 
     def wgrads(first, last):
         @pl.loop(first, last)
         def _(t):
             cols = pl.ds(pl.multiple_of(t * 512, 128), 512)
-            both = mm(lhs[0 : 2 * FP, :], rows[0, :, cols])
+            both = mm(lhs[0 : 2 * FL, :], rows[0, :, cols])
             o_gg[:, cols] = both[0:FL].astype(BF)
-            o_gu[:, cols] = both[FP : FP + FL].astype(BF)
-            o_gd[:, cols] = mm(lhs[2 * FP : 3 * FP, :], rows[1, :, cols])[0:FL].astype(BF)
-
-    pack_c()
+            o_gu[:, cols] = both[FL : 2 * FL].astype(BF)
+            o_gd[:, cols] = mm(lhs[2 * FL : 3 * FL, :], rows[1, :, cols]).astype(BF)
+
+    pack_c(0)
     go_c(0)
-    pack_n()
+    for k in range(1, NC):
+        choose(0, k)
+        pack_c(k)
     sent_c(0)
     go_c(1)
+    for k in range(NC):
+        choose(1, k)
+    pack_n()
     arrive_c(0)
-    turn_weights(0)
-    turn_weights(1)
     sent_c(1)
     go_c(2)
     go_c(3)
+    turn_weights(0)
     arrive_c(1)
+    go_n(0)
+    turn_weights(1)
     turn_weights(2)
+    relay(0)
     sent_c(2)
     sent_c(3)
-    go_n(0)
     go_n(1)
+    relay(1)
     arrive_c(2)
     arrive_c(3)
-    relay(0)
-    relay(1)
-    go_n(2)
-    go_n(3)
     unpack(0, 0)
-    hidden(0, 0)
-    terms(0, 0)
-    relay(2)
-    z_reduce(0, 0)
-    relay(3)
+    hidden(*EX[0][:2])
+    terms(*EX[0])
+    reduce_side(0)
     arrive_n(0)
     arrive_n(1)
+    go_n(2)
+    relay(2)
+    unpack(1, 0)
+    hidden(*EX[2][:2])
+    go_n(3)
+    relay(3)
+    terms(*EX[2])
     unpack(0, 1)
-    hidden(0, 1)
-    terms(0, 1)
-    unpack(1, 0)
-    z_reduce(0, 1)
-    hidden(1, 0)
-    terms(1, 0)
+    come_ex(2)
+    reduce_far(0)
+    go_far(0)
+    reduce_far(1)
+    hidden(*EX[1][:2])
+    go_far(1)
+    terms(*EX[1])
     arrive_n(2)
+    unpack(1, 1, (0,))
+    reduce_side(1)
+    hidden(*EX[3][:2])
     arrive_n(3)
-    z_reduce(1, 0)
-    unpack(1, 1)
-    hidden(1, 1)
-    terms(1, 1)
-    z_reduce(1, 1)
-    z_come(0)
+    terms(*EX[3])
     give_back(0)
+    come_ex(3)
+    reduce_far(2)
+    go_far(2)
+    unpack(1, 1, (1,))
     give_back(1)
+    hidden(*EX[4][:2])
+    terms(*EX[4])
     turn_rows()
+    come_ex(4)
+    reduce_far(3)
+    go_far(3)
+    give_back(2)
     wgrads(0, 5)
-    z_come(1)
-    give_back(2)
     give_back(3)
     wgrads(5, 10)
     for k in range(NC):
         collect(k)
-    o_in[...] = mm(lhs[3 * FP :, :], unp[...]).astype(BF)
-
-    for k in range(NC):
-        sent_n(k)
-    for k in range(NC):
-        sent(k, back)
-        for w in range(2):
-            z_forward(k, w).wait_send()
-            core_c(k, c, w).wait_send()
-        core_n(k, c).wait_send()
-        core_ex(k).wait_send()
-    for pair in range(2):
-        for w in range(2):
-            z_side_copy(pair, w).wait_send()
-        z_far_copy(pair).wait_send()
+    total()
+    def drain():
+        for k in range(NC):
+            sent_n(k)
+        for k in range(NC):
+            sent(k, back)
+            for w in range(2):
+                z_forward(k, w).wait_send()
+                core_c(k, c, w).wait_send()
+            core_n(k, c).wait_send()
+        for pair in range(2):
+            for w in range(2):
+                z_side_copy(pair, w).wait_send()
+        for k in range(NC):
+            z_far_copy(k).wait_send()
+        for ex in EX:
+            core_ex(*ex).wait_send()
+
+    drain()
 
 
 def hand_over(n, *refs):
     src, dst, sem = refs[:n], refs[n : 2 * n], refs[2 * n]
-    outs = [
-        pltpu.make_async_copy(src[i], dst[i] if i == 0 else dst[i].at[0], sem.at[i]) for i in range(n)
-    ]
+    outs = []
+    for i in range(n):
+        to = dst[i] if i == 0 else dst[i].at[0]
+        part = src[i].shape[0] // PARTS
+        for p in range(PARTS):
+            at = pl.ds(p * part, part)
+            outs.append(pltpu.make_async_copy(src[i].at[at], to.at[at], sem.at[i * PARTS + p]))
     for cp in outs:
         cp.start()
     for cp in outs:
@@ -443,12 +478,12 @@
         pltpu.VMEM((N_EXP, TOK), F32), bf(ALL, TOK), bf(M, M), bf(M, D),
         bf(NC * M, Q), bf(NC * M, E8), bf(2, NC * M, Q), bf(NC * M, E8), bf(2, 2, NC * M, E8),
         bf(2, ALL, D), pltpu.VMEM((2, 2, R, Q), F32), bf(NC, 2, R, Q), bf(NC, 2, R, Q),
-        bf(2, 2, R, Q), bf(2, 2, R, Q), bf(2, R, Q), bf(2, R, Q), bf(NC * M, E8), bf(NC * M, E8), bf(ALL, Q),
-        bf(ALL, 2 * FP), bf(ALL, FP), bf(4 * FP, ALL),
+        bf(2, 2, R, Q), bf(2, 2, R, Q), bf(NC, B, Q), bf(NC, B, Q), bf(NC * M, E8), bf(NC * M, E8), bf(ALL, Q),
+        bf(ALL, 2 * FP), bf(ALL, FP), bf(3 * FL + TOK, ALL),
         S((4,)), S((3,)),
         S((NC * G,)), S((NC * G,)), S((NC * G,)), S((NC * G,)),
         S((NC * 2,)), S((NC * 2,)), S((NC,)), S((NC,)), S((NC * 2,)), S((NC * 2,)),
-        S((NC,)), S((NC,)), S((4,)), S((4,)), S((2,)), S((2,)), S((NC * G,)), S((NC * G,)),
+        S((len(EX),)), S((len(EX),)), S((4,)), S((4,)), S((NC,)), S((NC,)), S((NC * G,)), S((NC * G,)),
     ]
     made = lambda *shape: jax.ShapeDtypeStruct(shape, BF)
     made_here = pl.pallas_call(
@@ -467,7 +502,7 @@
         out_shape=(made(TOK, Q), made(1, FL, D), made(1, FL, D), made(1, FL, D)),
         in_specs=[vmem] * 4,
         out_specs=(hbm,) * 4,
-        scratch_shapes=[S((4,))],
+        scratch_shapes=[S((4 * PARTS,))],
         compiler_params=pltpu.CompilerParams(vmem_limit_bytes=2 * 2**20),
                 cost_estimate=pl.CostEstimate(flops=0, bytes_accessed=7 * 10**6, transcendentals=0),
     )(*[pltpu.with_memory_space_constraint(a, pltpu.VMEM) for a in made_here])

time: 81.3 us -> 74.8 us (0.920)
  Pallas kernels: 79.8 us -> 74 us
    pallas_call x1, Pallas kernels: 77 us -> 71.1 us  [per_device(): pl.pallas_call(kernel, out_shape=(bf(TOK, Q), bf(FL, D), bf(FL, D), bf(FL...]
where the time goes in v3:
time: 74.8 us; the launch traced here: 74.6 us
  Pallas kernels  74 us (99%)
    pallas_call x1, Pallas kernels, per_device(): pl.pallas_call(kernel, out_shape=(bf(TOK, Q), bf(FL, D), bf(FL, D), bf(FL...  71.1 us
    pallas_call x1, Pallas kernels, per_device(): pl.pallas_call(functools.partial(hand_over, 4), out_shape=(made(TOK, Q),...  2.88 us

profile of v3, /device:TPU:1, one launch (start us, length us, event | category | flops | bytes accessed | tf_op | source)
XLA Modules:
  0.0 74.6 jit_solution(14597763709345614786)
XLA Ops:
  0.6 71.1 %shard_map.93 = (bf16[256,1280]{1,0:T(8,128)(2,1)S(1)}, bf16[192,5120]{1,0:T(8,128)(2,1)S(1)}, bf16[192,5120]{1,0:T(8,128)(2,1)S(1)}, bf16[192,5120]{1,0:T(8,128)(2,1)S(1)}) custom-call(bf16[256,5120]{1,0:T(8,128)(2,1)} %tok_hbm.1, bf16[256,5120]{1,0:T(8,128)(2,1)} %grad_hbm.1, s32[6,256]{1,0:T(8,128)} %bitcast.9, bf16[1,192,5120]{2,1,0:T(8,128)(2,1)} %bitcast.5, ...), custom_call_target="tpu_custom_call" | custom-call | flops 8000000000 | bytes 15000000 | tf_op jit(solution)/shard_map/pallas_call | solution.py:489
  71.8 2.9 %shard_map.94 = (bf16[256,1280]{1,0:T(8,128)(2,1)}, bf16[1,192,5120]{2,1,0:T(8,128)(2,1)}, bf16[1,192,5120]{2,1,0:T(8,128)(2,1)}, bf16[1,192,5120]{2,1,0:T(8,128)(2,1)}) custom-call(bf16[256,1280]{1,0:T(8,128)(2,1)S(1)} %get-tuple-element.12.refs_0_, bf16[192,5120]{1,0:T(8,128)(2,1)S(1)} %get-tuple-element.13.refs_1_, ...), custom_call_target="tpu_custom_call" | custom-call | bytes 7000000 | tf_op jit(solution)/shard_map/pallas_call | solution.py:500

commit v4 on v3

--- a/solution.py
+++ b/solution.py
@@ -15,10 +15,10 @@
 N_EXP = 32
 PARTS = 4
 CHUNKS = (
+    ((1, 0), (3, 0), (0, 1), (0, 3)),
+    ((1, 2), (3, 2), (2, 1), (2, 3)),
     ((1, 1), (3, 3), (1, 3), (3, 1)),
     ((2, 0), (0, 2), (0, 0), (2, 2)),
-    ((1, 2), (3, 2), (2, 1), (2, 3)),
-    ((1, 0), (3, 0), (0, 1), (0, 3)),
 )
 NC = len(CHUNKS)
 G = 4
@@ -407,18 +407,18 @@
     reduce_far(1)
     hidden(*EX[1][:2])
     go_far(1)
+    arrive_n(2)
     terms(*EX[1])
-    arrive_n(2)
     unpack(1, 1, (0,))
     reduce_side(1)
     hidden(*EX[3][:2])
     arrive_n(3)
     terms(*EX[3])
     give_back(0)
+    unpack(1, 1, (1,))
     come_ex(3)
     reduce_far(2)
     go_far(2)
-    unpack(1, 1, (1,))
     give_back(1)
     hidden(*EX[4][:2])
     terms(*EX[4])

time: 74.8 us -> 75.4 us (level); the launches traced: 74.6 us -> 74.4 us
  no operation moved by 1% of the time
where the time goes in v4:
time: 75.4 us; the launch traced here: 74.4 us
  Pallas kernels  73.6 us (98%)
  between operations  0.8 us (1%)
    pallas_call x1, Pallas kernels, per_device(): pl.pallas_call(kernel, out_shape=(bf(TOK, Q), bf(FL, D), bf(FL, D), bf(FL...  70.7 us
    pallas_call x1, Pallas kernels, per_device(): pl.pallas_call(functools.partial(hand_over, 4), out_shape=(made(TOK, Q),...  2.88 us

profile of v4, /device:TPU:1, one launch (start us, length us, event | category | flops | bytes accessed | tf_op | source)
XLA Modules:
  0.0 74.4 jit_solution(6681548309623354760)
XLA Ops:
  0.6 70.7 %shard_map.93 = (bf16[256,1280]{1,0:T(8,128)(2,1)S(1)}, bf16[192,5120]{1,0:T(8,128)(2,1)S(1)}, bf16[192,5120]{1,0:T(8,128)(2,1)S(1)}, bf16[192,5120]{1,0:T(8,128)(2,1)S(1)}) custom-call(bf16[256,5120]{1,0:T(8,128)(2,1)} %tok_hbm.1, bf16[256,5120]{1,0:T(8,128)(2,1)} %grad_hbm.1, s32[6,256]{1,0:T(8,128)} %bitcast.9, bf16[1,192,5120]{2,1,0:T(8,128)(2,1)} %bitcast.5, ...), custom_call_target="tpu_custom_call" | custom-call | flops 8000000000 | bytes 15000000 | tf_op jit(solution)/shard_map/pallas_call | solution.py:489
  71.3 2.9 %shard_map.94 = (bf16[256,1280]{1,0:T(8,128)(2,1)}, bf16[1,192,5120]{2,1,0:T(8,128)(2,1)}, bf16[1,192,5120]{2,1,0:T(8,128)(2,1)}, bf16[1,192,5120]{2,1,0:T(8,128)(2,1)}) custom-call(bf16[256,1280]{1,0:T(8,128)(2,1)S(1)} %get-tuple-element.12.refs_0_, bf16[192,5120]{1,0:T(8,128)(2,1)S(1)} %get-tuple-element.13.refs_1_, ...), custom_call_target="tpu_custom_call" | custom-call | bytes 7000000 | tf_op jit(solution)/shard_map/pallas_call | solution.py:500

commit v5 on v4

--- a/solution.py
+++ b/solution.py
@@ -397,7 +397,6 @@
     relay(2)
     unpack(1, 0)
     hidden(*EX[2][:2])
-    go_n(3)
     relay(3)
     terms(*EX[2])
     unpack(0, 1)
@@ -405,6 +404,7 @@
     reduce_far(0)
     go_far(0)
     reduce_far(1)
+    go_n(3)
     hidden(*EX[1][:2])
     go_far(1)
     arrive_n(2)

time: 75.4 us -> 72.9 us (0.967)
  Pallas kernels: 73.6 us -> 71.1 us
    pallas_call x1, Pallas kernels: 70.7 us -> 68.2 us  [per_device(): pl.pallas_call(kernel, out_shape=(bf(TOK, Q), bf(FL, D), bf(FL, D), bf(FL...]
where the time goes in v5:
time: 72.9 us; the launch traced here: 71.9 us
  Pallas kernels  71.1 us (98%)
  between operations  0.8 us (1%)
    pallas_call x1, Pallas kernels, per_device(): pl.pallas_call(kernel, out_shape=(bf(TOK, Q), bf(FL, D), bf(FL, D), bf(FL...  68.2 us
    pallas_call x1, Pallas kernels, per_device(): pl.pallas_call(functools.partial(hand_over, 4), out_shape=(made(TOK, Q),...  2.88 us

profile of v5, /device:TPU:1, one launch (start us, length us, event | category | flops | bytes accessed | tf_op | source)
XLA Modules:
  0.0 71.9 jit_solution(2094242301756590773)
XLA Ops:
  0.6 68.2 %shard_map.93 = (bf16[256,1280]{1,0:T(8,128)(2,1)S(1)}, bf16[192,5120]{1,0:T(8,128)(2,1)S(1)}, bf16[192,5120]{1,0:T(8,128)(2,1)S(1)}, bf16[192,5120]{1,0:T(8,128)(2,1)S(1)}) custom-call(bf16[256,5120]{1,0:T(8,128)(2,1)} %tok_hbm.1, bf16[256,5120]{1,0:T(8,128)(2,1)} %grad_hbm.1, s32[6,256]{1,0:T(8,128)} %bitcast.9, bf16[1,192,5120]{2,1,0:T(8,128)(2,1)} %bitcast.5, ...), custom_call_target="tpu_custom_call" | custom-call | flops 8000000000 | bytes 15000000 | tf_op jit(solution)/shard_map/pallas_call | solution.py:489
  68.8 2.9 %shard_map.94 = (bf16[256,1280]{1,0:T(8,128)(2,1)}, bf16[1,192,5120]{2,1,0:T(8,128)(2,1)}, bf16[1,192,5120]{2,1,0:T(8,128)(2,1)}, bf16[1,192,5120]{2,1,0:T(8,128)(2,1)}) custom-call(bf16[256,1280]{1,0:T(8,128)(2,1)S(1)} %get-tuple-element.12.refs_0_, bf16[192,5120]{1,0:T(8,128)(2,1)S(1)} %get-tuple-element.13.refs_1_, ...), custom_call_target="tpu_custom_call" | custom-call | bytes 7000000 | tf_op jit(solution)/shard_map/pallas_call | solution.py:500
